TPU v7x, 256 devices: a whole 4x4x8 slice. The times are simulated.
256 devices in a mesh: inst: 8 (over z_lo, core), tp: 32 (over x, y, z_hi).
Axes of the slice: x: 4, y: 4, z: 8 (z_hi: 2, z_lo: 4; z = z_hi * 4 + z_lo), core: 2. Of those that a mesh axis runs over, the one named last changes fastest.
Arguments:
- queries: bfloat16 [32, 8192], P('inst', 'tp')
- new_kv: bfloat16 [32, 2048], P('inst'), may hold values from -6 to 6
- kv_cache: bfloat16 [32, 4096, 2048], P('inst', 'tp')
- lengths: int32 [32], replicated, may hold values from 2 to 4096, as said below
- move_from: int32 [32], replicated, may hold values from 0 to 31, as said below
- o_weight: bfloat16 [8192, 8192], P('tp'), may hold values from -0.125 to 0.125
Outputs:
- attended: bfloat16 [32, 8192], P('inst', 'tp')
- new_cache: bfloat16 [32, 4096, 2048], P('inst', 'tp')
Inputs may be any that keep to these rules, and one draw needn't show every extreme that they name: `move_from`: a permutation of the 32 requests; slot g lies on instance g // 4; 3 requests leave each instance and 3 arrive at each, each from a different instance, so that from one instance to one other instance at most one request moves. `lengths`: some request has length 2 and some the full 4096.
All inputs are finite; a program needn't handle non-finite values.
Results may differ from a plain program's by a relative error of at most 0.0051.
Values may be sent and summed in bfloat16 or wider, within the bound.
A program may use at most 64 MiB of HBM per device.

v0:
```python
import jax
import jax.numpy as jnp
from jax import lax
from jax.sharding import PartitionSpec as P

QH = 64
KVH = 8
HD = 128


def joined(shard, axis, combine):
    everything = jax.tree.map(lambda part: lax.all_gather(part, axis), shard)
    initial = jax.tree.map(lambda part: part[0], everything)

    def step(k, so_far):
        return combine(so_far, jax.tree.map(lambda part: part[k], everything))

    return lax.fori_loop(1, lax.axis_size(axis), step, initial)


def combine_parts(first, second):
    first_max, first_total, first_sum = first
    second_max, second_total, second_sum = second
    larger = jnp.maximum(first_max, second_max)
    first_factor = jnp.exp(first_max - larger)
    second_factor = jnp.exp(second_max - larger)
    return (
        larger,
        first_total * first_factor + second_total * second_factor,
        first_sum * first_factor[..., None] + second_sum * second_factor[..., None],
    )


def on_device(queries, new_kv, kv_cache, lengths, move_from, o_weight):
    slot_count = kv_cache.shape[0]
    part_len = kv_cache.shape[1]
    kv_width = KVH * HD
    group_size = QH // KVH
    score_scale = HD ** (-0.5)
    inst_count = lax.axis_size("inst")
    inst_here = lax.axis_index("inst")
    source_all = (move_from // slot_count).reshape(inst_count, slot_count)
    anchor_all = (move_from % slot_count).reshape(inst_count, slot_count)
    chosen = (source_all == inst_here) & (
        jnp.arange(inst_count, dtype=jnp.int32)[:, None] != inst_here
    )
    picked = jnp.sum(jnp.where(chosen, anchor_all, 0), axis=1)
    outgoing = jnp.where(
        jnp.any(chosen, axis=1)[:, None, None],
        jnp.take(kv_cache, picked, axis=0),
        jnp.zeros((), kv_cache.dtype),
    )
    slot_from = lax.dynamic_slice_in_dim(move_from, inst_here * slot_count, slot_count)
    slot_source = slot_from // slot_count
    slot_anchor = slot_from % slot_count
    arrived = lax.all_to_all(outgoing, "inst", split_axis=0, concat_axis=0, tiled=True)
    remote = slot_count + slot_source
    lookup = jnp.concatenate([kv_cache, arrived], axis=0)
    slot_index = jnp.where(slot_source == inst_here, slot_anchor, remote)
    new_cache = jnp.take(lookup, slot_index, axis=0)
    slot_length = jnp.take(lengths, slot_from)
    all_queries = lax.all_gather(queries, "tp", axis=1, tiled=True)
    tp_rank = lax.axis_index("tp")
    tp_count = lax.axis_size("tp")
    head_count = QH // tp_count
    key_rows = new_cache[:, :, :kv_width].reshape(slot_count, part_len, KVH, HD)
    value_rows = new_cache[:, :, kv_width:].reshape(slot_count, part_len, KVH, HD)
    query_rows = all_queries.reshape(slot_count, KVH, group_size, HD)
    scores = (
        jnp.einsum("rhgd,rphd->rhgp", query_rows, key_rows, preferred_element_type=jnp.float32)
        * score_scale
    )
    position = tp_rank * part_len + jnp.arange(part_len, dtype=jnp.int32)
    usable = (position[None, :] < slot_length[:, None])[:, None, None, :]
    masked = jnp.where(usable, scores, -1e30)
    block_max = jnp.max(masked, axis=-1)
    weights = jnp.where(usable, jnp.exp(masked - block_max[..., None]), 0.0)
    block_total = jnp.sum(weights, axis=-1)
    block_sum = jnp.einsum(
        "rhgp,rphd->rhgd",
        weights.astype(jnp.bfloat16),
        value_rows,
        preferred_element_type=jnp.float32,
    )
    block_max = block_max.reshape(slot_count, QH)
    block_total = block_total.reshape(slot_count, QH)
    block_sum = block_sum.reshape(slot_count, QH, HD)
    merged_max, merged_total, merged_sum = joined(
        (block_max, block_total, block_sum), "tp", combine_parts
    )
    head_start = tp_rank * head_count
    part_max = lax.dynamic_slice_in_dim(merged_max, head_start, head_count, 1)
    part_total = lax.dynamic_slice_in_dim(merged_total, head_start, head_count, 1)
    part_sum = lax.dynamic_slice_in_dim(merged_sum, head_start, head_count, 1)
    own_queries = queries.reshape(slot_count, head_count, HD).astype(jnp.float32)
    kv_heads = (tp_rank * head_count + jnp.arange(head_count, dtype=jnp.int32)) // group_size
    new_keys = jnp.take(new_kv[:, :kv_width].reshape(slot_count, KVH, HD), kv_heads, axis=1).astype(
        jnp.float32
    )
    new_values = jnp.take(
        new_kv[:, kv_width:].reshape(slot_count, KVH, HD), kv_heads, axis=1
    ).astype(jnp.float32)
    own_score = jnp.sum(own_queries * new_keys, axis=-1) * score_scale
    highest = jnp.maximum(part_max, own_score)
    old_part = jnp.exp(part_max - highest)
    new_part = jnp.exp(own_score - highest)
    attention = (part_sum * old_part[..., None] + new_part[..., None] * new_values) / (
        part_total * old_part + new_part
    )[..., None]
    attention = attention.astype(jnp.bfloat16).reshape(slot_count, head_count * HD)
    partial_out = jnp.dot(attention, o_weight, preferred_element_type=jnp.float32)
    summed_all = lax.psum(partial_out, "tp")
    column_count = partial_out.shape[1] // tp_count
    attended = lax.dynamic_slice_in_dim(summed_all, tp_rank * column_count, column_count, 1).astype(
        jnp.bfloat16
    )
    return (attended, new_cache)


def solution(mesh):
    in_specs = (P("inst", "tp"), P("inst", None), P("inst", "tp", None), P(), P(), P("tp", None))
    out_specs = (P("inst", "tp"), P("inst", "tp", None))
    return jax.shard_map(
        on_device, mesh=mesh, in_specs=in_specs, out_specs=out_specs, check_vma=False
    )
```

profile of v0, /device:TPU:96, one launch (start us, length us, event | category | flops | bytes accessed | tf_op | source)
XLA Modules:
  0.0 711.5 jit_solution(16703016091490908090)
XLA Ops:
  9.1 4.3 gather_fusion.1
  13.4 4.6 select_select_fusion
  18.1 5.5 all-to-all-start
  24.4 173.7 %all_gather.12 = bf16[4,8192]{1,0:T(4,128)(2,1)S(1)} all-gather(bf16[4,256]{1,0:T(4,128)(2,1)S(1)} %copy-done.4), channel_id=1, replica_groups=mesh['inst'=8,'tp'=32] {'tp'}, dimensions={1}, use_global_device_ids=true | all-gather | bytes 67584 | tf_op jit(solution)/shard_map/all_gather | solution.py:62
  198.3 5.4 pad_maximum_fusion
  203.7 4.8 gather_fusion.2
  208.5 1.9 broadcast_select_fusion
  210.4 1.7 fusion.34
  212.1 1.6 copy.16
  213.7 2.3 copy.18
  216.5 2.6 convolution_bitcast_fusion
  220.8 116.1 %all_gather.14 = f32[32,4,64]{2,1,0:T(4,128)S(1)} all-gather(f32[1,4,64]{2,1,0:T(4,128)S(1)} %all_gather_reshape.10), channel_id=1, replica_groups=mesh['inst'=8,'tp'=32] {'tp'}, dimensions={0}, use_global_device_ids=true | all-gather | bytes 33792 | tf_op jit(solution)/shard_map/all_gather | solution.py:12
  336.9 107.0 %all_gather.13 = f32[32,4,64]{2,1,0:T(4,128)S(1)} all-gather(f32[1,4,64]{2,1,0:T(4,128)S(1)} %all_gather_reshape.9), channel_id=1, replica_groups=mesh['inst'=8,'tp'=32] {'tp'}, dimensions={0}, use_global_device_ids=true | all-gather | bytes 33792 | tf_op jit(solution)/shard_map/all_gather | solution.py:12
  444.8 34.8 %while.19 = (s32[]{:T(128)}, f32[4,64]{1,0:T(4,128)S(1)}, f32[4,64]{1,0:T(4,128)S(1)}, f32[4,64,128]{2,1,0:T(8,128)S(1)}, f32[32,4,64]{2,1,0:T(4,128)S(1)}, /*in...) while((s32[]{:T(128)}, f32[4,64]{1,0:T(4,128)S(1)}, ...), condition=%wide.region_5.6_spmd, body=%wide.region_4.5_spmd.sunk | while | flops 99845 | bytes 403607 | solution.py:18
  444.9 1.1 fusion.42
  446.0 1.1 fusion.42
  447.1 1.1 fusion.42
  448.3 1.1 fusion.42
  449.4 1.1 fusion.42
  450.5 1.1 fusion.42
  451.6 1.1 fusion.42
  452.7 1.1 fusion.42
  453.9 1.1 fusion.42
  462.8 1.1 fusion.42
  464.0 1.1 fusion.42
  465.1 1.1 fusion.42
  466.2 1.1 fusion.42
  467.3 1.1 fusion.42
  468.4 1.1 fusion.42
  469.6 1.1 fusion.42
  479.9 2.9 fusion.15
  482.8 221.2 %all-reduce.1 = bf16[4,8192]{1,0:T(4,128)(2,1)S(1)} all-reduce(f32[4,8192]{1,0:T(4,128)S(1)} %fusion.15), channel_id=1, replica_groups=mesh['inst'=8,'tp'=32] {'tp'}, use_global_device_ids=true, to_apply=%region_7.9 | all-reduce | flops 32768 | bytes 196608 | tf_op jit(solution)/shard_map/psum | solution.py:112
  (99 shorter events, 23.8 us)
Async XLA Ops:
  7.2 16.6 %copy-start = (s32[32]{0:T(128)S(1)}, s32[32]{0:T(128)}, u32[]{:S(2)}) copy-start(s32[32]{0:T(128)} %param.13) | copy-start | bytes 388
  18.1 5.5 copy-start.5
  18.1 6.3 copy-start.4
  18.1 180.2 %copy-start.1 = (bf16[4,128,2048]{2,1,0:T(8,128)(2,1)S(1)}, bf16[4,128,2048]{2,1,0:T(8,128)(2,1)}, u32[]{:S(2)}) copy-start(bf16[4,128,2048]{2,1,0:T(8,128)(2,1)} %param.12) | copy-start | bytes 6291460
  18.1 180.2 %all-to-all-start = ((bf16[8,128,2048]{2,1,0:T(8,128)(2,1)}), bf16[8,128,2048]{2,1,0:T(8,128)(2,1)}, u32[]{:S(2)}, u32[]{:S(2)}) async-start(bf16[8,128,2048]{2,1,0:T(8,128)(2,1)} %select_select_fusion), calls=%async_computation | async-start | bytes 8388608 | tf_op jit(solution)/shard_map/all_to_all | solution.py:56
  23.6 420.3 %all-gather.2.cloned.1.call-start = ((), (), s32[]{:S(2)}) async-start(), calls=%async_computation.1 | async-start | bytes 4325376 | tf_op jit(solution)/shard_map/all_gather | solution.py:12
  210.3 5.7 copy-start.2
  212.1 7.0 copy-start.3
Sparse Core Ops, SparseCore 0:
  219.2 104.3 all-gather.1
where the time goes:
time: 713 us; the launch traced here: 711 us
  blocking collectives  618 us (87%)
  other arithmetic  48.4 us (7%)
  local copies, waits for them, and re-layouts  18.7 us (3%)
  between operations  14.2 us (2%)
    all_gather x2, blocking collectives, joined(): everything = jax.tree.map(lambda part: lax.all_gather(part, axis), shard)  223 us
    psum x1, blocking collectives, on_device(): summed_all = lax.psum(partial_out, 'tp')  221 us
    all_gather x1, blocking collectives, on_device(): all_queries = lax.all_gather(queries, 'tp', axis=1, tiled=True)  174 us
    add x31, other arithmetic, combine_parts(): first_sum * first_factor[..., None] + second_sum * second_factor[..., None]  33.2 us
  transfers between devices with their start and end apart: 2, of which 0 were waited for; matrix products, arithmetic and copies ran while one was open for 0% of the time, Pallas kernels for 0%

commit v1 on v0

v1 whole, which is shorter than its diff:
```python
import functools

import jax
import jax.numpy as jnp
from jax import lax
from jax.experimental import pallas as pl
from jax.experimental.pallas import tpu as pltpu
from jax.sharding import PartitionSpec as P

MESH = pl.DeviceIdType.MESH
KVH = 8
HD = 128
SCALE = HD ** -0.5
STEPS = (6, 7, 8, 9, 12)
PIECES = 4
ROWS = 16
F32 = jnp.float32
BF16 = jnp.bfloat16

SEND, PLACE, SLOT_OF, LENGTH, SOURCE, ONCHIP, DUMP = 0, 32, 40, 44, 48, 52, 63


def plan_kernel(move_ref, len_ref, tab_ref, pick_ref, slot_of, count, rank, par, free):
    inst = lax.axis_index("inst")
    chip = inst // 2
    for n in range(64):
        tab_ref[n] = 0
    for n in range(32):
        tab_ref[SEND + n] = -1
        slot_of[move_ref[n]] = n
    for n in range(16):
        count[n] = 0
    for r in range(32):
        kind = (r // 8) * 4 + lax.shift_right_logical(slot_of[r], 3)
        seen = count[kind]
        rank[r] = seen
        count[kind] = seen + 1
    most = jnp.int32(STEPS[0])
    for d in range(2):

        def number(a, b):
            return count[a * 4 + b] if d == 0 else count[(3 - a) * 4 + 3 - b]

        n02, n03, n12, n13 = number(0, 2), number(0, 3), number(1, 2), number(1, 3)
        o0, o1 = n02 + n03, n12 + n13
        par[d * 8 + 0] = n03
        par[d * 8 + 1] = o0
        par[d * 8 + 2] = n13
        one = jnp.int32(1)
        mask = lax.shift_left(lax.shift_left(one, n03) - 1, jnp.int32(2))
        again = lax.shift_left(lax.shift_left(one, jnp.maximum(n13 - 1, 0)) - 1, o0 + 2)
        mask = mask | jnp.where(n13 > 0, again | 2, 0)
        seen = jnp.int32(0)
        for s in range(10):
            free[d * 16 + seen] = s
            seen = seen + 1 - (lax.shift_right_logical(mask, jnp.int32(s)) & 1)
        most = jnp.maximum(most, o0 + jnp.maximum(o1, jnp.minimum(o0, 1)))
        most = jnp.maximum(most, jnp.where(n13 > 1, o0 + n13 + 1, 0))
    pick = jnp.int32(0)
    for steps in STEPS[:-1]:
        pick = pick + (most > steps).astype(jnp.int32)
    pick_ref[0] = pick

    def first_step(r, a_chip, b_chip):
        d = (b_chip < a_chip).astype(jnp.int32)
        a = jnp.where(d == 1, 3 - a_chip, a_chip)
        b = jnp.where(d == 1, 3 - b_chip, b_chip)
        k = rank[r]
        n03, o0, n13 = par[d * 8], par[d * 8 + 1], par[d * 8 + 2]
        p0 = k + jnp.where(b == 3, 0, jnp.where(b == 2, n03, o0))
        q = jnp.where(b == 3, k, n13 + k)
        p1 = jnp.where(q == 0, 0, o0 + q)
        p2 = free[d * 16 + k]
        return d, jnp.where(a == 0, p0, jnp.where(a == 1, p1, p2)), b - a

    for q in range(8):
        r = chip * 8 + q
        b = lax.shift_right_logical(slot_of[r], 3)
        d, step, _ = first_step(r, chip, b)
        tab_ref[jnp.where(b == chip, DUMP, SEND + d * 16 + step)] = q
    for k in range(4):
        r = inst * 4 + k
        g = slot_of[r]
        home = lax.shift_right_logical(g, 2)
        tab_ref[jnp.where((home != inst) & (home // 2 == chip), ONCHIP, DUMP)] = k
        tab_ref[SLOT_OF + k] = g
        tab_ref[LENGTH + k] = len_ref[r]
    for j in range(4):
        r = move_ref[inst * 4 + j]
        home = lax.shift_right_logical(r, 2)
        a = lax.shift_right_logical(r, 3)
        d, step, hops = first_step(r, a, chip)
        arrival = 8 + d * 16 + step + hops - 1
        tab_ref[PLACE + j] = jnp.where(home == inst, r & 3, jnp.where(a == chip, 4, arrival))
        tab_ref[SOURCE + j] = r


def main_kernel(
    steps, tab, q_ref, new_ref, cache, weight, attended, arrived, onchip,
    own, part, tx, rx, on_stage, w_buf,
    a_send, a_buf, b_send, b_buf, d_send, d_buf, e_send, e_buf, h_send, h_buf, i_send, i_buf, j_send, j_buf,
    tx_sem, rx_sem, mir_send, mir_recv, keep_sem, part_send, part_recv, on_sem, load_sem,
    a_ss, a_rs, b_ss, b_rs, d_ss, d_rs, e_sem, h_ss, h_rs, i_sem, j_ss, j_rs,
):
    inst = lax.axis_index("inst")
    tp = lax.axis_index("tp")
    chip, core = inst // 2, inst % 2
    zh, u = tp % 2, tp // 2
    me = zh * 8 + inst
    partner = {"inst": chip * 2 + 1 - core}
    z_partner = {"tp": u * 2 + 1 - zh}

    def peer16(d):
        e = (me + d) % 16
        return {"inst": e % 8, "tp": u * 2 + e // 8}

    def peer_xy(d):
        return {"tp": ((u + d) % 16) * 2 + zh}

    def remote(src, dst, ss, rs, to):
        return pltpu.make_async_remote_copy(
            src_ref=src, dst_ref=dst, send_sem=ss, recv_sem=rs, device_id=to, device_id_type=MESH
        )

    half = pl.multiple_of(core * 64, 64)
    other = pl.multiple_of(64 - core * 64, 64)
    loads = [
        pltpu.make_async_copy(cache, own, load_sem.at[0]),
        pltpu.make_async_copy(weight, w_buf, load_sem.at[1]),
    ]
    for load in loads:
        load.start()

    barrier = pltpu.get_barrier_semaphore()
    for d in range(1, 16):
        pl.semaphore_signal(barrier, inc=1, device_id=peer16(d), device_id_type=MESH)
        pl.semaphore_signal(barrier, inc=1, device_id=peer_xy(d), device_id_type=MESH)
    pl.semaphore_wait(barrier, 30)

    shares = [
        remote(
            cache.at[:, pl.ds(pl.multiple_of(other + p * ROWS, ROWS), ROWS)],
            part[p], part_send.at[p], part_recv.at[p], partner,
        )
        for p in range(PIECES)
    ]
    for share in shares:
        share.start()

    def has_in(d):
        return chip > 0 if d == 0 else chip < 3

    def has_out(d):
        return chip < 3 if d == 0 else chip > 0

    def hop(d, s, p):
        to = {"inst": jnp.clip(inst + (2 if d == 0 else -2), 0, 7)}
        rows = pl.ds(p * ROWS, ROWS)
        return remote(tx.at[d, s, rows], rx.at[d, s, rows], tx_sem.at[d, s, p], rx_sem.at[d, s, p], to)

    def mirror(d, s, p0, count):
        rows = pl.ds(p0 * ROWS, count * ROWS)
        there = pl.ds(pl.multiple_of(half + p0 * ROWS, ROWS), count * ROWS)
        src = rx.at[d, s, rows]
        dst = arrived.at[d, s, there]
        return (
            remote(src, dst, mir_send.at[d, s, p0], mir_recv.at[d, s, p0], partner),
            pltpu.make_async_copy(src, dst, keep_sem.at[d, s, p0]),
        )

    def migrate(s, p, first):
        rows = pl.ds(p * ROWS, ROWS)
        if first:
            shares[p].wait_recv()
        own_rows = pl.ds(pl.multiple_of(half + p * ROWS, ROWS), ROWS)
        for d in range(2):
            if not first:

                @pl.when(has_in(d))
                def _():
                    hop(d, s - 1, p).wait_recv()

            @pl.when(has_out(d))
            def _():
                code = tab[SEND + d * 16 + s]
                choice = jnp.maximum(code, 0)
                mine = lax.shift_right_logical(choice, 2) == core
                index = choice & 3
                block = jnp.where(mine, own[index, own_rows, :], part[p][index])
                if not first:
                    block = jnp.where(code < 0, rx[d, s - 1, rows, :], block)
                tx[d, s, rows, :] = block
                hop(d, s, p).start()

            if not first and p == PIECES - 1:

                @pl.when(has_in(d))
                def _():
                    for copy in mirror(d, s - 1, 0, PIECES):
                        copy.start()

    def end_piece(p):
        for d in range(2):

            @pl.when(has_in(d))
            def _():
                hop(d, steps - 1, p).wait_recv()
                for copy in mirror(d, steps - 1, p, 1):
                    copy.start()

    row16 = lax.broadcasted_iota(jnp.int32, (16, 1), 0)

    def by_slot(kind, values):
        out = jnp.full(kind.shape, values[0], jnp.int32)
        for k in range(1, 4):
            out = jnp.where(kind == k, values[k], out)
        return out

    def a_copy(d):
        return remote(a_send, a_buf.at[me], a_ss.at[d - 1], a_rs.at[d - 1], peer16(d))

    def a_take(d):
        return remote(a_send, a_buf.at[(me + 16 - d) % 16], a_ss.at[d - 1], a_rs.at[d - 1], peer16(d))

    def stage_a():
        lanes = pl.ds(pl.multiple_of((u // 2) * HD, HD), HD)
        value_lanes = pl.ds(pl.multiple_of(KVH * HD + (u // 2) * HD, HD), HD)
        q = q_ref[...].astype(F32)
        packed = jnp.concatenate(
            [q[:, :HD], q[:, HD:], new_ref[:, lanes].astype(F32), new_ref[:, value_lanes].astype(F32)], axis=0
        ).astype(BF16)
        a_send[...] = packed
        a_buf[pl.ds(me, 1)] = packed[None]
        for d in range(1, 16):
            a_copy(d).start()

    def xy_copy(send, buf, ss, rs, d, whole):
        src = send if whole else send.at[(u + d) % 16]
        return remote(src, buf.at[u], ss.at[d - 1], rs.at[d - 1], peer_xy(d))

    def xy_take(send, buf, ss, rs, d, whole):
        src = send if whole else send.at[(u + d) % 16]
        return remote(src, buf.at[(u + 16 - d) % 16], ss.at[d - 1], rs.at[d - 1], peer_xy(d))

    def stage_b():
        for d in range(1, 16):
            a_take(d).wait_recv()
        blocks, spots = [], []
        for k in range(4):
            g = tab[SLOT_OF + k]
            spots.append(g & 3)
            for z in range(2):
                blocks.append(a_buf[z * 8 + lax.shift_right_logical(g, 2)])
        stacked = jnp.concatenate(blocks, axis=0)
        row = lax.broadcasted_iota(jnp.int32, (48, 128), 0)
        col = lax.broadcasted_iota(jnp.int32, (48, 128), 1)
        inner = row % 16
        k, h, group = inner // 4, inner % 4, row // 16
        spot = by_slot(k, spots)
        place = jnp.where(
            group == 0, (k * 2 + h // 2) * 16 + (h % 2) * 4, k * 32 + 4 + group * 4
        )
        chosen = (col == place + spot).astype(F32).astype(BF16)
        picked = jnp.dot(chosen, stacked, preferred_element_type=F32)
        mine = picked[:16].astype(BF16)
        b_send[...] = mine
        b_buf[pl.ds(u, 1)] = mine[None]
        for d in range(1, 16):
            xy_copy(b_send, b_buf, b_ss, b_rs, d, True).start()
        return picked

    def wait_b():
        for d in range(1, 16):
            xy_take(b_send, b_buf, b_ss, b_rs, d, True).wait_recv()

    row32 = lax.broadcasted_iota(jnp.int32, (32, 1), 0)
    of_row = (row32 % 16) // 4

    def stage_c(heads):
        limit = by_slot(of_row, [tab[LENGTH + k] for k in range(4)])
        position = tp * 128 + lax.broadcasted_iota(jnp.int32, (32, 128), 1)
        usable = position < limit
        for k in heads:
            query = b_buf[2 * k : 2 * k + 2].reshape(32, HD)
            keys = own[:, :, k * HD : (k + 1) * HD].reshape(512, HD)
            values = own[:, :, (KVH + k) * HD : (KVH + k + 1) * HD].reshape(512, HD)
            full = lax.dot_general(query, keys, (((1,), (1,)), ((), ())), preferred_element_type=F32)
            scores = full[:, :128]
            for r in range(1, 4):
                scores = jnp.where(of_row == r, full[:, r * 128 : (r + 1) * 128], scores)
            masked = jnp.where(usable, scores * SCALE, -1e30)
            top = jnp.max(masked, axis=1, keepdims=True)
            weights = jnp.where(usable, jnp.exp(masked - top), 0.0)
            total = jnp.sum(weights, axis=1, keepdims=True)
            spread = jnp.concatenate(
                [jnp.where(of_row == r, weights, 0.0).astype(BF16) for r in range(4)], axis=1
            )
            summed = jnp.dot(spread, values, preferred_element_type=F32)
            lane = lax.broadcasted_iota(jnp.int32, (32, HD), 1)
            stats = jnp.where(lane < 64, top, total)
            d_send[2 * k : 2 * k + 2] = jnp.concatenate([summed, stats], axis=1).reshape(2, 16, 2 * HD)

    def send_d():
        d_buf[pl.ds(u, 1)] = d_send[pl.ds(u, 1)]
        for d in range(1, 16):
            xy_copy(d_send, d_buf, d_ss, d_rs, d, False).start()

    def merge(blocks):
        tops = [block[:, HD : HD + 1] for block in blocks]
        top = functools.reduce(jnp.maximum, tops)
        factors = [jnp.exp(t - top) for t in tops]
        summed = sum(block[:, :HD] * f for block, f in zip(blocks, factors))
        total = sum(block[:, HD + 64 : HD + 65] * f for block, f in zip(blocks, factors))
        return top, total, summed

    def e_copy():
        return remote(e_send, e_buf, e_sem.at[0], e_sem.at[1], z_partner)

    def stage_d():
        for d in range(1, 16):
            xy_take(d_send, d_buf, d_ss, d_rs, d, False).wait_recv()
        top, total, summed = merge([d_buf[n] for n in range(16)])
        lane = lax.broadcasted_iota(jnp.int32, (16, HD), 1)
        e_send[...] = jnp.concatenate([summed, jnp.where(lane < 64, top, total)], axis=1)
        e_copy().start()

    def stage_e(picked):
        e_copy().wait_recv()
        top, total, summed = merge([e_send[...], e_buf[...]])
        query, key, value = picked[:16], picked[16:32], picked[32:48]
        own_score = jnp.sum(query * key, axis=1, keepdims=True) * SCALE
        highest = jnp.maximum(top, own_score)
        old, new = jnp.exp(top - highest), jnp.exp(own_score - highest)
        attention = ((summed * old + new * value) / (total * old + new)).astype(BF16)
        row = lax.broadcasted_iota(jnp.int32, (16, 16), 0)
        col = lax.broadcasted_iota(jnp.int32, (16, 16), 1)
        heads = []
        for h in range(2):
            chosen = ((col == (row % 4) * 4 + zh * 2 + h) & (row < 8)).astype(F32).astype(BF16)
            heads.append(jnp.dot(chosen, attention, preferred_element_type=F32))
        both = jnp.concatenate(heads, axis=1)
        low = jnp.where(row16 < 4, both, 0.0).astype(BF16)
        high = jnp.where(row16 >= 4, both, 0.0).astype(BF16)
        return low, high

    def stage_f(low, high, first, last):
        for n in range(first, last):
            at = n * 512
            out = jnp.dot(low, w_buf[:, at : at + 256], preferred_element_type=F32)
            out = out + jnp.dot(high, w_buf[:, at + 256 : at + 512], preferred_element_type=F32)
            h_send[n] = out[:8]

    def send_h():
        h_buf[pl.ds(u, 1)] = h_send[pl.ds(u, 1)]
        for d in range(1, 16):
            xy_copy(h_send, h_buf, h_ss, h_rs, d, False).start()

    def i_copy():
        return remote(i_send, i_buf, i_sem.at[0], i_sem.at[1], z_partner)

    def stage_h():
        for d in range(1, 16):
            xy_take(h_send, h_buf, h_ss, h_rs, d, False).wait_recv()
        i_send[...] = sum(h_buf[n] for n in range(16))
        i_copy().start()

    def j_copy(d):
        return remote(j_send, j_buf.at[inst], j_ss.at[d - 1], j_rs.at[d - 1], {"inst": (inst + d) % 8})

    def j_take(d):
        return remote(
            j_send, j_buf.at[(inst + 8 - d) % 8], j_ss.at[d - 1], j_rs.at[d - 1], {"inst": (inst + d) % 8}
        )

    def stage_i():
        i_copy().wait_recv()
        total = i_send[...] + i_buf[...]
        total = jnp.where(zh == 0, total[:4], total[4:])
        packed = jnp.concatenate([total[:, :HD], total[:, HD:]], axis=0)
        j_send[...] = packed
        j_buf[pl.ds(inst, 1)] = packed[None]
        for d in range(1, 8):
            j_copy(d).start()

    def stage_j():
        for d in range(1, 8):
            j_take(d).wait_recv()
        row8 = lax.broadcasted_iota(jnp.int32, (8, HD), 0)
        rows = []
        for j in range(4):
            r = tab[SOURCE + j]
            block = jnp.where(row8 % 4 == (r & 3), j_buf[lax.shift_right_logical(r, 2)], 0.0)
            pair = [jnp.sum(block[4 * n : 4 * n + 4], axis=0, keepdims=True) for n in range(2)]
            rows.append(jnp.concatenate(pair, axis=1))
        attended[...] = jnp.concatenate(rows, axis=0).astype(BF16)

    stage_a()
    loads[0].wait()
    for p in range(PIECES):
        migrate(0, p, True)

    on_stage[...] = own[tab[ONCHIP]]
    on_copy = remote(on_stage, onchip, on_sem.at[0], on_sem.at[1], partner)
    on_copy.start()

    migrate(1, 0, False)
    picked = stage_b()
    migrate(1, 1, False)
    migrate(1, 2, False)
    migrate(1, 3, False)
    migrate(2, 0, False)
    wait_b()
    for p in range(4):
        stage_c((2 * p, 2 * p + 1))
        if p < 3:
            migrate(2, p + 1, False)
    send_d()
    migrate(3, 0, False)
    migrate(3, 1, False)
    migrate(3, 2, False)
    stage_d()
    migrate(3, 3, False)
    migrate(4, 0, False)
    migrate(4, 1, False)
    low, high = stage_e(picked)
    loads[1].wait()
    stage_f(low, high, 0, 8)
    migrate(4, 2, False)
    stage_f(low, high, 8, 16)
    send_h()
    migrate(4, 3, False)
    migrate(5, 0, False)
    migrate(5, 1, False)
    migrate(5, 2, False)
    stage_h()
    migrate(5, 3, False)

    def more(s, carry):
        for p in range(PIECES):
            migrate(s, p, False)
        return carry

    if steps > 6:
        for p in range(PIECES):
            migrate(6, p, False)
            if p == 2:
                stage_i()
        if steps > 7:
            lax.fori_loop(7, steps, more, 0)
    end_piece(0)
    end_piece(1)
    if steps == 6:
        stage_i()
    end_piece(2)
    end_piece(3)
    stage_j()

    for p in range(PIECES):
        shares[p].wait_send()
    on_copy.wait()
    for d in range(1, 16):
        a_copy(d).wait_send()
        xy_copy(b_send, b_buf, b_ss, b_rs, d, True).wait_send()
        xy_copy(d_send, d_buf, d_ss, d_rs, d, False).wait_send()
        xy_copy(h_send, h_buf, h_ss, h_rs, d, False).wait_send()
    e_copy().wait_send()
    i_copy().wait_send()
    for d in range(1, 8):
        j_copy(d).wait_send()

    def drain(s, carry):
        for d in range(2):

            @pl.when(has_out(d))
            def _():
                for p in range(PIECES):
                    hop(d, s, p).wait_send()

        return carry

    lax.fori_loop(0, steps, drain, 0)

    def drain_mirror(s, carry):
        for d in range(2):

            @pl.when(has_in(d))
            def _():
                there, here = mirror(d, s, 0, PIECES)
                there.wait()
                here.wait()

        return carry

    lax.fori_loop(0, steps - 1, drain_mirror, 0)
    for d in range(2):

        @pl.when(has_in(d))
        def _():
            for p in range(PIECES):
                there, here = mirror(d, steps - 1, p, 1)
                there.wait()
                here.wait()


def place_kernel(tab, cache, arrived, onchip, out, sems):
    for j in range(4):
        code = tab[PLACE + j]

        @pl.when(code < 4)
        def _():
            pltpu.make_async_copy(cache.at[jnp.minimum(code, 3)], out.at[j], sems.at[j]).start()

        @pl.when(code == 4)
        def _():
            pltpu.make_async_copy(onchip, out.at[j], sems.at[j]).start()

        @pl.when(code > 4)
        def _():
            at = jnp.maximum(code - 8, 0)
            step = jnp.minimum(at & 15, arrived.shape[1] - 1)
            src = arrived.at[lax.shift_right_logical(at, 4), step]
            pltpu.make_async_copy(src, out.at[j], sems.at[j]).start()

    for j in range(4):
        pltpu.make_async_copy(onchip, out.at[j], sems.at[j]).wait()


def variant(number, tab, queries, new_kv, kv_cache, o_weight):
    steps = STEPS[number]
    sem = pltpu.SemaphoreType.DMA
    vmem = pltpu.VMEM
    anywhere = pl.BlockSpec(memory_space=pl.ANY)
    smem = pl.BlockSpec(memory_space=pltpu.SMEM)
    whole = pl.BlockSpec(memory_space=pltpu.VMEM)
    request = kv_cache.shape[1:]
    attended, arrived, onchip = pl.pallas_call(
        functools.partial(main_kernel, steps),
        out_shape=(
            jax.ShapeDtypeStruct((4, 256), BF16),
            jax.ShapeDtypeStruct((2, steps) + request, BF16),
            jax.ShapeDtypeStruct(request, BF16),
        ),
        in_specs=[smem, whole, whole, anywhere, anywhere],
        out_specs=(whole, anywhere, anywhere),
        scratch_shapes=[
            vmem((4, 128, 2048), BF16),
            [vmem((4, ROWS, 2048), BF16) for _ in range(PIECES)],
            vmem((2, steps, 64, 2048), BF16),
            vmem((2, steps, 64, 2048), BF16),
            vmem((128, 2048), BF16),
            vmem((256, 8192), BF16),
            vmem((16, HD), BF16), vmem((16, 16, HD), BF16),
            vmem((16, HD), BF16), vmem((16, 16, HD), BF16),
            vmem((16, 16, 2 * HD), F32), vmem((16, 16, 2 * HD), F32),
            vmem((16, 2 * HD), F32), vmem((16, 2 * HD), F32),
            vmem((16, 8, 256), F32), vmem((16, 8, 256), F32),
            vmem((8, 256), F32), vmem((8, 256), F32),
            vmem((8, HD), F32), vmem((8, 8, HD), F32),
            sem((2, steps, PIECES)), sem((2, steps, PIECES)),
            sem((2, steps, PIECES)), sem((2, steps, PIECES)), sem((2, steps, PIECES)),
            sem((PIECES,)), sem((PIECES,)), sem((2,)), sem((2,)),
            sem((15,)), sem((15,)), sem((15,)), sem((15,)), sem((15,)), sem((15,)),
            sem((2,)), sem((15,)), sem((15,)), sem((2,)), sem((7,)), sem((7,)),
        ],
        compiler_params=pltpu.CompilerParams(
            collective_id=number, has_side_effects=True, vmem_limit_bytes=48 * 2**20
        ),
        name="migrate_and_attend",
    )(tab, queries, new_kv, kv_cache, o_weight)
    new_cache = pl.pallas_call(
        place_kernel,
        out_shape=jax.ShapeDtypeStruct(kv_cache.shape, BF16),
        in_specs=[smem, anywhere, anywhere, anywhere],
        out_specs=anywhere,
        scratch_shapes=[sem((4,))],
        name="place",
    )(tab, kv_cache, arrived, onchip)
    return attended, new_cache


def on_device(queries, new_kv, kv_cache, lengths, move_from, o_weight):
    smem = pl.BlockSpec(memory_space=pltpu.SMEM)
    words = functools.partial(pltpu.SMEM, dtype=jnp.int32)
    tab, pick = pl.pallas_call(
        plan_kernel,
        out_shape=(jax.ShapeDtypeStruct((64,), jnp.int32), jax.ShapeDtypeStruct((1,), jnp.int32)),
        in_specs=[smem, smem],
        out_specs=(smem, smem),
        scratch_shapes=[words((32,)), words((16,)), words((32,)), words((16,)), words((32,))],
        name="plan",
    )(move_from, lengths)
    branches = [functools.partial(variant, n) for n in range(len(STEPS))]
    return lax.switch(pick[0], branches, tab, queries, new_kv, kv_cache, o_weight)


def solution(mesh):
    in_specs = (P("inst", "tp"), P("inst", None), P("inst", "tp", None), P(), P(), P("tp", None))
    out_specs = (P("inst", "tp"), P("inst", "tp", None))
    return jax.shard_map(
        on_device, mesh=mesh, in_specs=in_specs, out_specs=out_specs, check_vma=False
    )
```

time: 713 us -> 113 us (0.16)
  the two profiles are of different devices: /device:TPU:96 before, /device:TPU:1 now
where the time goes in v1:
time: 113 us
  Pallas kernels  110 us (97%)
  local copies, waits for them, and re-layouts  1.38 us (1%)
  between operations  1.3 us (1%)
    pallas_call x1, Pallas kernels, variant(): pl.pallas_call(functools.partial(main_kernel, steps), out_shape=(jax.Shap...  58.8 us
    pallas_call x1, Pallas kernels, variant(): pl.pallas_call(place_kernel, out_shape=jax.ShapeDtypeStruct(kv_cache.shap...  49.3 us

profile of v1, /device:TPU:1, one launch (start us, length us, event | category | flops | bytes accessed | tf_op | source)
XLA Modules:
  0.0 112.8 jit_solution(16853788194761777630)
XLA Ops:
  0.6 1.7 %plan.1 = (s32[64]{0:T(128)S(1)}, s32[1]{0:T(128)}) custom-call(s32[32]{0:T(128)} %move_ref.1, s32[32]{0:T(128)} %len_ref.1), custom_call_target="tpu_custom_call" | custom-call | tf_op jit(solution)/shard_map/plan/pallas_call | solution.py:584
  3.0 109.3 %conditional.1 = (bf16[4,256]{1,0:T(4,128)(2,1)S(1)}, bf16[4,128,2048]{2,1,0:T(8,128)(2,1)}) conditional(s32[]{:T(128)} %bitcast, (s32[64]{0:T(128)S(1)}, bf16[4,256]{1,0:T(4,128)(2,1)}, bf16[4,2048]{1,0:T(4,128)(2,1)}, bf16[4,128,2048]{2,1,0:T(8,128)(2,1)}, bf16[256,8192]{1,0:T(8,128)(2,1)}) %tuple.27, ...), branch_computations={%region_0.0_spmd, %region_1.0_spmd, %region_2.0_spmd, %region_3.0_... | conditional | bytes 10485832 | solution.py:593
  3.0 0.0 copy-start.5
  3.0 58.8 %migrate_and_attend.5 = (bf16[4,256]{1,0:T(4,128)(2,1)S(1)}, bf16[2,6,128,2048]{3,2,1,0:T(8,128)(2,1)}, bf16[128,2048]{1,0:T(8,128)(2,1)S(1)}) custom-call(s32[64]{0:T(128)S(1)} %get-tuple-element.50.tab, bf16[4,256]{1,0:T(4,128)(2,1)} %get-tuple-element.51.q_ref, bf16[4,2048]{1,0:T(4,128)(2,1)} %get-tuple-element.52.new_ref, ...), custom_call_target="tpu_custom_call" | custom-call | tf_op jit(solution)/shard_map/cond/branch_0_fun/migrate_and_attend/pallas_call | solution.py:536
  61.8 0.0 copy-start
  61.8 0.8 copy-done
  62.6 0.0 copy-done.5
  62.6 49.3 %place.5 = bf16[4,128,2048]{2,1,0:T(8,128)(2,1)} custom-call(s32[64]{0:T(128)S(1)} %get-tuple-element.50.tab, bf16[4,128,2048]{2,1,0:T(8,128)(2,1)S(1)} %copy-done.5, bf16[2,6,128,2048]{3,2,1,0:T(8,128)(2,1)} %get-tuple-element.56.arrived, bf16[128,2048]{1,0:T(8,128)(2,1)} %copy-done), custom_call_target="tpu_custom_call" | custom-call | tf_op jit(solution)/shard_map/cond/branch_0_fun/place/pallas_call | solution.py:570
  112.2 0.6 copy.24
Async XLA Ops:
  3.0 59.6 %copy-start.5 = (bf16[4,128,2048]{2,1,0:T(8,128)(2,1)S(1)}, bf16[4,128,2048]{2,1,0:T(8,128)(2,1)}, u32[]{:S(2)}) copy-start(bf16[4,128,2048]{2,1,0:T(8,128)(2,1)} %get-tuple-element.53.cache) | copy-start | bytes 6291460 | tf_op jit(solution)/shard_map/cond
  61.8 0.8 copy-start
